TPU v7x, 32 devices: a whole 2x2x4 slice. The times are simulated.
32 devices in a mesh: section: 4 (over y, x), ctx: 8 (over z, core).
Axes of the slice: x: 2, y: 2, z: 4, core: 2. Of those that a mesh axis runs over, the one named last changes fastest.
Arguments:
- projected: bfloat16 [4, 3072, 3072], P('section', 'ctx'), may hold values from -64 to 64
- grad_out: bfloat16 [4, 3072, 3072], P('section', 'ctx'), may hold values from -6 to 6
- doc_lengths: int32 [7], replicated, may hold values from 1 to 768, as said below
Outputs:
- grad_kv: float32 [3072, 2048], P('ctx')
Inputs may be any that keep to these rules, and one draw needn't show every extreme that they name: `doc_lengths`: the lengths sum to 3072; the first document is shorter than 384 tokens and the second has exactly 768.
All inputs are finite; a program needn't handle non-finite values.
Results may differ from a plain program's by a relative error of at most 0.0031.
Values may be sent and summed in bfloat16 or wider, within the bound.
A program may use at most 128 MiB of HBM per device.

v0:
```python
import functools
import math

import jax
import jax.numpy as jnp
from jax import lax
from jax.experimental import pallas as pl
from jax.experimental.pallas import tpu as pltpu
from jax.sharding import PartitionSpec as P

HEAD_SIZE = 128
KV_HEAD_COUNT = 8
QUERY_PER_KV = 3
REACH = 2
ROWS = 128
AHEAD = 2
MASKED_SCORE = -1e30
MESH = pl.DeviceIdType.MESH


def ring_swap(place, sections):
    half = sections // 2
    back = place // half
    return place * (1 - back) + back * (half + sections - 1 - place)


def dot_last(left, right):
    return lax.dot_general(
        left, right, (((1,), (1,)), ((), ())), preferred_element_type=jnp.float32
    )


def folded(value, reduce):
    return reduce(value.reshape(-1, 8, value.shape[-1]), axis=0)


def kernel(
    sections,
    blocks,
    lengths_ref,
    projected_ref,
    grad_out_ref,
    out_ref,
    queries,
    cotangents,
    window,
    bias,
    score_buf,
    prob_grad_buf,
    halves,
    grads,
    pair_in,
    hop_out,
    hop_in,
    part_out,
    part_in,
    final_half,
    load_sem,
    lend_send,
    lend_recv,
    ring_send,
    ring_recv,
    hop_kv_send,
    hop_kv_recv,
    pair_kv_send,
    pair_kv_recv,
    pair_send,
    pair_recv,
    hop_send,
    hop_recv,
    part_send,
    part_recv,
    spread_send,
    spread_recv,
    store_sem,
):
    section = lax.axis_index("section")
    block = lax.axis_index("ctx")
    odd = lax.rem(block, 2)
    partner = block + 1 - 2 * odd
    place = ring_swap(section, sections)
    heads = KV_HEAD_COUNT
    tokens = out_ref.shape[0]
    width = heads * HEAD_SIZE
    group_width = QUERY_PER_KV * HEAD_SIZE
    span = REACH * tokens + ROWS
    scale = 1.0 / math.sqrt(HEAD_SIZE)
    exponent_scale = scale * math.log2(math.e)
    cross = section > 0
    others = sections - 1
    lent = heads // sections
    kept = heads - lent
    at_home = jnp.where(section == 0, 1, 0)
    has_before = block >= REACH
    has_after = block + REACH < blocks

    def block_rows(index):
        return pl.ds(index * tokens, tokens)

    def load_shared(head, kind):
        return pltpu.make_async_copy(
            projected_ref.at[:, pl.ds(kind * width + head * HEAD_SIZE, HEAD_SIZE)],
            window.at[head, kind, block_rows(REACH), :],
            load_sem.at[head, kind],
        )

    def load_group(head, kind):
        source, target = ((projected_ref, queries), (grad_out_ref, cotangents))[kind]
        return pltpu.make_async_copy(
            source.at[:, pl.ds(head * group_width, group_width)],
            target.at[head],
            load_sem.at[head, kind],
        )

    def lend_copy(index, kind, source):
        origin, target = ((projected_ref, queries), (grad_out_ref, cotangents))[kind]
        unit = index * others + source - 1
        return pltpu.make_async_remote_copy(
            src_ref=origin.at[:, pl.ds((kept + index) * group_width, group_width)],
            dst_ref=target.at[unit],
            send_sem=lend_send.at[index, kind],
            recv_sem=lend_recv.at[unit, kind],
            device_id={"section": 0, "ctx": block},
            device_id_type=MESH,
        )

    def owner_of(head):
        return (1 - head // kept) * (1 + lax.rem(head, others))

    def ring_copy(head, kind, way):
        target_place = lax.rem(place + 1 - 2 * way + sections, sections)
        own = window.at[head, kind, block_rows(REACH), :]
        return pltpu.make_async_remote_copy(
            src_ref=own,
            dst_ref=own,
            send_sem=ring_send.at[head, kind, way],
            recv_sem=ring_recv.at[head, kind],
            device_id={"section": ring_swap(target_place, sections), "ctx": block},
            device_id_type=MESH,
        )

    def ring_sends(kind, way):
        middle = sections // 2
        if way == 0:
            return place < middle if kind == 0 else place + 1 < middle
        above = lax.rem(place - 1 + sections, sections)
        starts = (place == 0) | (place > middle)
        return starts & (above > middle if kind == 0 else above >= middle)

    def ring_start(head, kind):
        for way in range(2):

            @pl.when(ring_sends(kind, way))
            def _():
                ring_copy(head, kind, way).start()

    def ring_sent(head):
        for kind in range(2):
            for way in range(2):

                @pl.when(ring_sends(kind, way))
                def _():
                    ring_copy(head, kind, way).wait_send()

    def to_block(source, target, send_sem, recv_sem, target_block):
        return pltpu.make_async_remote_copy(
            src_ref=source,
            dst_ref=target,
            send_sem=send_sem,
            recv_sem=recv_sem,
            device_id={"section": section, "ctx": target_block},
            device_id_type=MESH,
        )

    def hop_kv(head):
        return to_block(
            window.at[head, :, block_rows(REACH), :],
            window.at[head, :, block_rows(0), :],
            hop_kv_send.at[head],
            hop_kv_recv.at[head],
            block + REACH,
        )

    def pair_kv(head, source_block):
        return to_block(
            window.at[head, :, block_rows(source_block), :],
            window.at[head, :, block_rows(1), :],
            pair_kv_send.at[head],
            pair_kv_recv.at[head],
            partner,
        )

    def pair_grads(head):
        return to_block(
            grads.at[head, :, block_rows(1), :],
            pair_in.at[head],
            pair_send.at[head],
            pair_recv.at[head],
            partner,
        )

    def hop_grads(head):
        return to_block(
            hop_out.at[head], hop_in.at[head], hop_send.at[head], hop_recv.at[head], block - REACH
        )

    def part_copy(head, source, target):
        return pltpu.make_async_remote_copy(
            src_ref=part_out.at[head],
            dst_ref=part_in.at[head // others, source],
            send_sem=part_send.at[head],
            recv_sem=part_recv.at[head // others, source],
            device_id={"section": target, "ctx": block},
            device_id_type=MESH,
        )

    def out_columns(head, kind):
        start = pl.multiple_of(kind * width + head * HEAD_SIZE, HEAD_SIZE)
        return out_ref.at[:, pl.ds(start, HEAD_SIZE)]

    def spread_copy(head, kind, target):
        return pltpu.make_async_remote_copy(
            src_ref=final_half.at[head, kind],
            dst_ref=out_columns(head, kind),
            send_sem=spread_send.at[head, target, kind],
            recv_sem=spread_recv.at[head, kind],
            device_id={"section": target, "ctx": block},
            device_id_type=MESH,
        )

    def store_copy(head, kind):
        return pltpu.make_async_copy(
            final_half.at[head, kind],
            out_columns(head, kind),
            store_sem.at[head, kind],
        )

    @pl.when(section == 0)
    def _():
        for head in range(heads):
            for kind in range(2):
                load_shared(head, kind).start()

    @pl.when(cross)
    def _():
        for head in range(kept):
            for kind in range(2):
                load_group(head, kind).start()

    barrier = pltpu.get_barrier_semaphore()
    for step in range(1, sections):
        pl.semaphore_signal(
            barrier,
            inc=1,
            device_id={"section": lax.rem(section + step, sections), "ctx": block},
            device_id_type=MESH,
        )
    pl.semaphore_signal(
        barrier, inc=1, device_id={"section": section, "ctx": partner}, device_id_type=MESH
    )

    @pl.when(has_before)
    def _():
        pl.semaphore_signal(
            barrier,
            inc=1,
            device_id={"section": section, "ctx": block - REACH},
            device_id_type=MESH,
        )

    @pl.when(has_after)
    def _():
        pl.semaphore_signal(
            barrier,
            inc=1,
            device_id={"section": section, "ctx": block + REACH},
            device_id_type=MESH,
        )

    before_count = jnp.where(has_before, 1, 0)
    after_count = jnp.where(has_after, 1, 0)
    pl.semaphore_wait(barrier, sections + before_count + after_count)

    def finish(head):
        own = block_rows(REACH)
        for source in range(1, sections):

            @pl.when(cross & (section != source))
            def _():
                part_copy(head, source, section).wait_recv()
                grads[head, :, own, :] += part_in[head // others, source].astype(jnp.float32)

        final_half[head, 0] = (grads[head, 0, own, :] * scale).astype(jnp.bfloat16)
        final_half[head, 1] = grads[head, 1, own, :].astype(jnp.bfloat16)
        for kind in range(2):
            store_copy(head, kind).start()
            for step in range(1, sections):
                spread_copy(head, kind, lax.rem(section + step, sections)).start()

    def pass_across(head):
        @pl.when(has_before & (odd == 1))
        def _():
            hop_kv(head).wait_recv()
            pair_kv(head, 0).start()

    def to_later(head):
        @pl.when(has_after)
        def _():
            hop_kv(head).start()

        @pl.when(odd == 0)
        def _():
            pair_kv(head, REACH).start()

    @pl.when(section == 0)
    def _():
        for head in range(heads):
            for kind in range(2):
                load_shared(head, kind).wait()
        for head in range(min(3, kept)):
            for kind in range(2):
                ring_start(head, kind)
        for head in range(kept, heads):
            to_later(head)

    @pl.when(cross)
    def _():
        for index in range(lent):
            for kind in range(2):
                lend_copy(index, kind, section).start()

    for index in range(tokens // ROWS):
        query_place = block * tokens + index * ROWS + lax.broadcasted_iota(
            jnp.int32, (8, ROWS), 1
        )
        start = jnp.zeros((8, ROWS), jnp.int32)
        end = 0
        for document in range(lengths_ref.shape[0]):
            end = end + lengths_ref[document]
            start = jnp.where(query_place >= end, end, start)
        key_place = (
            (block - REACH) * tokens
            + index * ROWS
            + lax.broadcasted_iota(jnp.int32, (span, ROWS), 0)
        )
        allowed = (key_place >= start[:1]) & (key_place <= query_place[:1])
        bias[index] = jnp.where(allowed, 0.0, MASKED_SCORE)

    @pl.loop(0, heads)
    def _(head):
        grads[head] = jnp.zeros(grads.shape[1:], jnp.float32)

        @pl.when(block < REACH)
        def _():
            window[head, :, block_rows(0), :] = jnp.zeros((2, tokens, HEAD_SIZE), jnp.bfloat16)

        @pl.when(block == 0)
        def _():
            window[head, :, block_rows(1), :] = jnp.zeros((2, tokens, HEAD_SIZE), jnp.bfloat16)

    @pl.when(section == 0)
    def _():
        for head in range(min(3, kept), kept):
            for kind in range(2):
                ring_start(head, kind)
        for head in range(kept, heads):
            pass_across(head)

    @pl.when(cross)
    def _():
        for head in range(kept):
            for kind in range(2):
                load_group(head, kind).wait()

    def pass_on(head):
        for kind in range(2):
            ring_copy(head, kind, 0).wait_recv()
            ring_start(head, kind)

        to_later(head)

    def compute(unit, head):
        chunks = span // ROWS

        def stacked(array, index):
            rows = pl.ds(index * ROWS, ROWS)
            return jnp.concatenate(
                [
                    array[unit, rows, member * HEAD_SIZE : (member + 1) * HEAD_SIZE]
                    for member in range(QUERY_PER_KV)
                ],
                axis=0,
            )

        def products(index):
            band = pl.ds(index * ROWS, span)
            scores = dot_last(window[head, 0, band, :], stacked(queries, index))
            top = jnp.full((8, QUERY_PER_KV * ROWS), -3e38, jnp.float32)
            for chunk in range(chunks):
                here = pl.ds(chunk * ROWS, ROWS)
                mask = bias[index, here, :]
                score = scores[chunk * ROWS : (chunk + 1) * ROWS] + jnp.concatenate(
                    [mask] * QUERY_PER_KV, axis=1
                )
                score_buf[index, here, :] = score
                top = jnp.maximum(top, folded(score, jnp.max))
            prob_grad_buf[index] = dot_last(
                window[head, 1, band, :], stacked(cotangents, index)
            )
            return jnp.max(top, axis=0, keepdims=True)

        def soften(index, top):
            total = jnp.zeros((8, QUERY_PER_KV * ROWS), jnp.float32)
            delta = jnp.zeros((8, QUERY_PER_KV * ROWS), jnp.float32)
            for chunk in range(chunks):
                here = pl.ds(chunk * ROWS, ROWS)
                power = jnp.exp2((score_buf[index, here, :] - top) * exponent_scale)
                score_buf[index, here, :] = power
                total = total + folded(power, jnp.sum)
                delta = delta + folded(power * prob_grad_buf[index, here, :], jnp.sum)
            inverse = 1.0 / jnp.sum(total, axis=0, keepdims=True)
            delta = jnp.sum(delta, axis=0, keepdims=True) * inverse
            for chunk in range(chunks):
                here = pl.ds(chunk * ROWS, ROWS)
                prob = score_buf[index, here, :] * inverse
                score_grad = prob * (prob_grad_buf[index, here, :] - delta)
                halves[index, 0, here, :] = score_grad.astype(jnp.bfloat16)
                halves[index, 1, here, :] = prob.astype(jnp.bfloat16)

        def accumulate(index):
            for kind, array in enumerate((queries, cotangents)):
                update = jnp.dot(
                    halves[index, kind],
                    stacked(array, index),
                    preferred_element_type=jnp.float32,
                )
                grads[head, kind, pl.ds(index * ROWS, span), :] += update

        count = tokens // ROWS
        tops = [products(0)]
        for index in range(count):
            if index + 1 < count:
                tops.append(products(index + 1))
            soften(index, tops[index])
            accumulate(index)

    def head_of(unit):
        return (1 - at_home) * unit + at_home * (kept + unit // others)

    def attend(unit):
        head = head_of(unit)
        first = cross | (lax.rem(unit, others) == 0)
        last = cross | (lax.rem(unit, others) == others - 1)

        @pl.when(section == 0)
        def _():
            for kind in range(2):
                lend_copy(unit // others, kind, 1 + lax.rem(unit, others)).wait_recv()

        @pl.when(first & has_before & (odd == 0))
        def _():
            hop_kv(head).wait_recv()

        @pl.when(first & (has_before | (odd == 1)))
        def _():
            pair_kv(head, REACH).wait_recv()

        compute(unit, head)

        @pl.when(last & (has_before | (odd == 1)))
        def _():
            pair_grads(head).start()

    def send_back(head):
        @pl.when(has_before)
        def _():
            @pl.when(odd == 0)
            def _():
                hop_out[head] = grads[head, :, block_rows(0), :].astype(jnp.bfloat16)

            @pl.when(odd == 1)
            def _():
                pair_grads(head).wait_recv()
                hop_out[head] = (grads[head, :, block_rows(0), :] + pair_in[head]).astype(
                    jnp.bfloat16
                )

            hop_grads(head).start()

    def gather(head):
        @pl.when(odd == 0)
        def _():
            pair_grads(head).wait_recv()
            grads[head, :, block_rows(REACH), :] += pair_in[head]

        @pl.when(has_after)
        def _():
            hop_grads(head).wait_recv()
            grads[head, :, block_rows(REACH), :] += hop_in[head].astype(jnp.float32)

        owner = owner_of(head)

        @pl.when(owner != section)
        def _():
            part_out[head] = grads[head, :, block_rows(REACH), :].astype(jnp.bfloat16)
            part_copy(head, section, owner).start()

    @pl.loop(0, kept + AHEAD + 4)
    def _(step):
        def stage(lag, run):
            unit = step - lag

            @pl.when((unit >= 0) & (unit < kept))
            def _():
                run(unit)

        def when_summed(run):
            def staged(unit):
                @pl.when(cross | (lax.rem(unit, others) == others - 1))
                def _():
                    run(head_of(unit))

            return staged

        def when_cross(run):
            def staged(unit):
                @pl.when(cross)
                def _():
                    run(unit)

            return staged

        def finish_own(head):
            @pl.when(owner_of(head) == section)
            def _():
                finish(head)

        stage(0, when_cross(pass_on))
        stage(1, when_cross(pass_across))
        stage(AHEAD, attend)
        stage(AHEAD + 1, when_summed(send_back))
        stage(AHEAD + 2, when_summed(gather))
        stage(AHEAD + 3, when_summed(finish_own))

    @pl.loop(0, heads)
    def _(head):
        owner = owner_of(head)
        home = head // kept
        for kind in range(2):

            @pl.when(owner == section)
            def _():
                store_copy(head, kind).wait()
                for step in range(1, sections):
                    spread_copy(head, kind, lax.rem(section + step, sections)).wait_send()

            @pl.when(owner != section)
            def _():
                spread_copy(head, kind, owner).wait_recv()


        @pl.when(home == 0)
        def _():
            ring_sent(head)

        @pl.when(cross & (home == 1))
        def _():
            for kind in range(2):
                lend_copy(head - kept, kind, section).wait_send()

        @pl.when(home == at_home)
        def _():
            @pl.when(has_after)
            def _():
                hop_kv(head).wait_send()

            @pl.when(has_before | (odd == 0))
            def _():
                pair_kv(head, REACH).wait_send()

            @pl.when(has_before | (odd == 1))
            def _():
                pair_grads(head).wait_send()

            @pl.when(has_before)
            def _():
                hop_grads(head).wait_send()

            @pl.when(owner != section)
            def _():
                part_copy(head, section, owner).wait_send()


def on_device(projected, grad_out, doc_lengths):
    sections = lax.axis_size("section")
    blocks = lax.axis_size("ctx")
    tokens = projected.shape[1]
    heads = KV_HEAD_COUNT
    lent = heads // sections
    kept = heads - lent
    span = REACH * tokens + ROWS
    window_rows = (REACH + 1) * tokens
    group_width = QUERY_PER_KV * HEAD_SIZE
    bf16, f32 = jnp.bfloat16, jnp.float32
    dma = pltpu.SemaphoreType.DMA
    return pl.pallas_call(
        functools.partial(kernel, sections, blocks),
        out_shape=jax.ShapeDtypeStruct((tokens, 2 * heads * HEAD_SIZE), bf16),
        in_specs=[
            pl.BlockSpec(memory_space=pltpu.SMEM),
            pl.BlockSpec(memory_space=pl.ANY),
            pl.BlockSpec(memory_space=pl.ANY),
        ],
        out_specs=pl.BlockSpec(memory_space=pl.ANY),
        scratch_shapes=[
            pltpu.VMEM((kept, tokens, group_width), bf16),
            pltpu.VMEM((kept, tokens, group_width), bf16),
            pltpu.VMEM((heads, 2, window_rows, HEAD_SIZE), bf16),
            pltpu.VMEM((tokens // ROWS, span, ROWS), f32),
            pltpu.VMEM((tokens // ROWS, span, QUERY_PER_KV * ROWS), f32),
            pltpu.VMEM((tokens // ROWS, span, QUERY_PER_KV * ROWS), f32),
            pltpu.VMEM((tokens // ROWS, 2, span, QUERY_PER_KV * ROWS), bf16),
            pltpu.VMEM((heads, 2, window_rows, HEAD_SIZE), f32),
            pltpu.VMEM((heads, 2, tokens, HEAD_SIZE), f32),
            pltpu.VMEM((heads, 2, tokens, HEAD_SIZE), bf16),
            pltpu.VMEM((heads, 2, tokens, HEAD_SIZE), bf16),
            pltpu.VMEM((heads, 2, tokens, HEAD_SIZE), bf16),
            pltpu.VMEM((lent, sections, 2, tokens, HEAD_SIZE), bf16),
            pltpu.VMEM((heads, 2, tokens, HEAD_SIZE), bf16),
            dma((heads, 2)),
            dma((lent, 2)),
            dma((kept, 2)),
            dma((heads, 2, 2)),
            dma((heads, 2)),
            dma((heads,)),
            dma((heads,)),
            dma((heads,)),
            dma((heads,)),
            dma((heads,)),
            dma((heads,)),
            dma((heads,)),
            dma((heads,)),
            dma((heads,)),
            dma((lent, sections)),
            dma((heads, sections, 2)),
            dma((heads, 2)),
            dma((heads, 2)),
        ],
        compiler_params=pltpu.CompilerParams(
            collective_id=0, has_side_effects=True, vmem_limit_bytes=56 * 1024 * 1024
        ),
        cost_estimate=pl.CostEstimate(
            flops=10 * heads * tokens * group_width * span // 1,
            bytes_accessed=16 * tokens * heads * group_width,
            transcendentals=heads * QUERY_PER_KV * tokens * span,
        ),
    )(doc_lengths, projected[0], grad_out[0]).astype(f32)


def solution(mesh):
    return jax.shard_map(
        on_device,
        mesh=mesh,
        in_specs=(P("section", "ctx", None), P("section", "ctx", None), P()),
        out_specs=P("ctx", None),
        check_vma=False,
    )
```

profile of v0, /device:TPU:0, one launch (start us, length us, event | category | flops | bytes accessed | tf_op | source)
XLA Modules:
  0.0 90.9 jit_solution(7009137774197651837)
XLA Ops:
  0.0 87.5 %shard_map.37 = bf16[384,2048]{1,0:T(8,128)(2,1)} custom-call(s32[7]{0:T(128)} %lengths_ref.1, bf16[384,3072]{1,0:T(8,128)(2,1)} %bitcast.2, bf16[384,3072]{1,0:T(8,128)(2,1)} %bitcast.3), custom_call_target="tpu_custom_call" | custom-call | flops 10569646080 | bytes 18874368 | tf_op jit(solution)/shard_map/pallas_call | solution.py:606
  87.5 3.4 %convert_element_type.3 = f32[384,2048]{1,0:T(8,128)} convert(bf16[384,2048]{1,0:T(8,128)(2,1)} %shard_map.37) | non-fusion elementwise | flops 786432 | bytes 4718592 | tf_op jit(solution)/shard_map/convert_element_type | solution.py:657
where the time goes:
time: 91.1 us; the launch traced here: 90.9 us
  Pallas kernels  87.5 us (96%)
  other arithmetic  3.45 us (4%)
    pallas_call x1, Pallas kernels, on_device(): pl.pallas_call(functools.partial(kernel, sections, blocks), out_shape=jax...  87.5 us
    convert_element_type x1, other arithmetic, on_device(): return pl.pallas_call(functools.partial(kernel, sections, blocks), out_sh...  3.45 us

commit v1 on v0

--- a/solution.py
+++ b/solution.py
@@ -199,17 +199,21 @@
             partner,
         )
 
-    def hop_grads(head):
+    def hop_grads(head, kind):
         return to_block(
-            hop_out.at[head], hop_in.at[head], hop_send.at[head], hop_recv.at[head], block - REACH
-        )
-
-    def part_copy(head, source, target):
+            hop_out.at[head, kind],
+            hop_in.at[head, kind],
+            hop_send.at[head, kind],
+            hop_recv.at[head, kind],
+            block - REACH,
+        )
+
+    def part_copy(head, kind, source, target):
         return pltpu.make_async_remote_copy(
-            src_ref=part_out.at[head],
-            dst_ref=part_in.at[head // others, source],
-            send_sem=part_send.at[head],
-            recv_sem=part_recv.at[head // others, source],
+            src_ref=part_out.at[head, kind],
+            dst_ref=part_in.at[head // others, source, kind],
+            send_sem=part_send.at[head, kind],
+            recv_sem=part_recv.at[head // others, source, kind],
             device_id={"section": target, "ctx": block},
             device_id_type=MESH,
         )
@@ -283,16 +287,20 @@
 
     def finish(head):
         own = block_rows(REACH)
-        for source in range(1, sections):
-
-            @pl.when(cross & (section != source))
-            def _():
-                part_copy(head, source, section).wait_recv()
-                grads[head, :, own, :] += part_in[head // others, source].astype(jnp.float32)
-
-        final_half[head, 0] = (grads[head, 0, own, :] * scale).astype(jnp.bfloat16)
-        final_half[head, 1] = grads[head, 1, own, :].astype(jnp.bfloat16)
         for kind in range(2):
+            for source in range(1, sections):
+
+                @pl.when(cross & (section != source))
+                def _():
+                    part_copy(head, kind, source, section).wait_recv()
+                    grads[head, kind, own, :] += part_in[head // others, source, kind].astype(
+                        jnp.float32
+                    )
+
+            total = grads[head, kind, own, :]
+            if kind == 0:
+                total = total * scale
+            final_half[head, kind] = total.astype(jnp.bfloat16)
             store_copy(head, kind).start()
             for step in range(1, sections):
                 spread_copy(head, kind, lax.rem(section + step, sections)).start()
@@ -314,12 +322,13 @@
 
     @pl.when(section == 0)
     def _():
-        for head in range(heads):
+        for head in range(min(3, kept)):
             for kind in range(2):
                 load_shared(head, kind).wait()
-        for head in range(min(3, kept)):
-            for kind in range(2):
                 ring_start(head, kind)
+        for head in range(min(3, kept), heads):
+            for kind in range(2):
+                load_shared(head, kind).wait()
         for head in range(kept, heads):
             to_later(head)
 
@@ -474,36 +483,43 @@
     def send_back(head):
         @pl.when(has_before)
         def _():
-            @pl.when(odd == 0)
-            def _():
-                hop_out[head] = grads[head, :, block_rows(0), :].astype(jnp.bfloat16)
-
             @pl.when(odd == 1)
             def _():
                 pair_grads(head).wait_recv()
-                hop_out[head] = (grads[head, :, block_rows(0), :] + pair_in[head]).astype(
-                    jnp.bfloat16
-                )
-
-            hop_grads(head).start()
+
+            for kind in range(2):
+
+                @pl.when(odd == 0)
+                def _():
+                    hop_out[head, kind] = grads[head, kind, block_rows(0), :].astype(jnp.bfloat16)
+
+                @pl.when(odd == 1)
+                def _():
+                    hop_out[head, kind] = (
+                        grads[head, kind, block_rows(0), :] + pair_in[head, kind]
+                    ).astype(jnp.bfloat16)
+
+                hop_grads(head, kind).start()
 
     def gather(head):
+        owner = owner_of(head)
+
         @pl.when(odd == 0)
         def _():
             pair_grads(head).wait_recv()
             grads[head, :, block_rows(REACH), :] += pair_in[head]
 
-        @pl.when(has_after)
-        def _():
-            hop_grads(head).wait_recv()
-            grads[head, :, block_rows(REACH), :] += hop_in[head].astype(jnp.float32)
-
-        owner = owner_of(head)
-
-        @pl.when(owner != section)
-        def _():
-            part_out[head] = grads[head, :, block_rows(REACH), :].astype(jnp.bfloat16)
-            part_copy(head, section, owner).start()
+        for kind in range(2):
+
+            @pl.when(has_after)
+            def _():
+                hop_grads(head, kind).wait_recv()
+                grads[head, kind, block_rows(REACH), :] += hop_in[head, kind].astype(jnp.float32)
+
+            @pl.when(owner != section)
+            def _():
+                part_out[head, kind] = grads[head, kind, block_rows(REACH), :].astype(jnp.bfloat16)
+                part_copy(head, kind, section, owner).start()
 
     @pl.loop(0, kept + AHEAD + 4)
     def _(step):
@@ -584,11 +600,13 @@
 
             @pl.when(has_before)
             def _():
-                hop_grads(head).wait_send()
+                for kind in range(2):
+                    hop_grads(head, kind).wait_send()
 
             @pl.when(owner != section)
             def _():
-                part_copy(head, section, owner).wait_send()
+                for kind in range(2):
+                    part_copy(head, kind, section, owner).wait_send()
 
 
 def on_device(projected, grad_out, doc_lengths):
@@ -638,10 +656,10 @@
             dma((heads,)),
             dma((heads,)),
             dma((heads,)),
-            dma((heads,)),
-            dma((heads,)),
-            dma((heads,)),
-            dma((lent, sections)),
+            dma((heads, 2)),
+            dma((heads, 2)),
+            dma((heads, 2)),
+            dma((lent, sections, 2)),
             dma((heads, sections, 2)),
             dma((heads, 2)),
             dma((heads, 2)),

time: 91.1 us -> 91.5 us (level)
  no operation moved by 1% of the time
where the time goes in v1:
time: 91.5 us; the launch traced here: 91.3 us
  Pallas kernels  87.9 us (96%)
  other arithmetic  3.45 us (4%)
    pallas_call x1, Pallas kernels, on_device(): pl.pallas_call(functools.partial(kernel, sections, blocks), out_shape=jax...  87.9 us
    convert_element_type x1, other arithmetic, on_device(): return pl.pallas_call(functools.partial(kernel, sections, blocks), out_sh...  3.45 us

profile of v1, /device:TPU:0, one launch (start us, length us, event | category | flops | bytes accessed | tf_op | source)
XLA Modules:
  0.0 91.3 jit_solution(15912343589328787957)
XLA Ops:
  0.0 87.9 %shard_map.37 = bf16[384,2048]{1,0:T(8,128)(2,1)} custom-call(s32[7]{0:T(128)} %lengths_ref.1, bf16[384,3072]{1,0:T(8,128)(2,1)} %bitcast.2, bf16[384,3072]{1,0:T(8,128)(2,1)} %bitcast.3), custom_call_target="tpu_custom_call" | custom-call | flops 10569646080 | bytes 18874368 | tf_op jit(solution)/shard_map/pallas_call | solution.py:624
  87.9 3.4 %convert_element_type.3 = f32[384,2048]{1,0:T(8,128)} convert(bf16[384,2048]{1,0:T(8,128)(2,1)} %shard_map.37) | non-fusion elementwise | flops 786432 | bytes 4718592 | tf_op jit(solution)/shard_map/convert_element_type | solution.py:675

commit v2 on v1

--- a/solution.py
+++ b/solution.py
@@ -334,9 +334,8 @@
 
     @pl.when(cross)
     def _():
-        for index in range(lent):
-            for kind in range(2):
-                lend_copy(index, kind, section).start()
+        for kind in range(2):
+            lend_copy(0, kind, section).start()
 
     for index in range(tokens // ROWS):
         query_place = block * tokens + index * ROWS + lax.broadcasted_iota(
@@ -553,6 +552,13 @@
 
         stage(0, when_cross(pass_on))
         stage(1, when_cross(pass_across))
+        for index in range(1, lent):
+
+            @pl.when(cross & (step == AHEAD + index - 1))
+            def _():
+                for kind in range(2):
+                    lend_copy(index, kind, section).start()
+
         stage(AHEAD, attend)
         stage(AHEAD + 1, when_summed(send_back))
         stage(AHEAD + 2, when_summed(gather))

time: 91.5 us -> 91.5 us (level)
  no operation moved by 1% of the time
where the time goes in v2:
time: 91.5 us; the launch traced here: 91.3 us
  Pallas kernels  87.9 us (96%)
  other arithmetic  3.45 us (4%)
    pallas_call x1, Pallas kernels, on_device(): pl.pallas_call(functools.partial(kernel, sections, blocks), out_shape=jax...  87.9 us
    convert_element_type x1, other arithmetic, on_device(): return pl.pallas_call(functools.partial(kernel, sections, blocks), out_sh...  3.45 us

profile of v2, /device:TPU:0, one launch (start us, length us, event | category | flops | bytes accessed | tf_op | source)
XLA Modules:
  0.0 91.3 jit_solution(4631395740786949950)
XLA Ops:
  0.0 87.9 %shard_map.37 = bf16[384,2048]{1,0:T(8,128)(2,1)} custom-call(s32[7]{0:T(128)} %lengths_ref.1, bf16[384,3072]{1,0:T(8,128)(2,1)} %bitcast.2, bf16[384,3072]{1,0:T(8,128)(2,1)} %bitcast.3), custom_call_target="tpu_custom_call" | custom-call | flops 10569646080 | bytes 18874368 | tf_op jit(solution)/shard_map/pallas_call | solution.py:630
  87.9 3.4 %convert_element_type.3 = f32[384,2048]{1,0:T(8,128)} convert(bf16[384,2048]{1,0:T(8,128)(2,1)} %shard_map.37) | non-fusion elementwise | flops 786432 | bytes 4718592 | tf_op jit(solution)/shard_map/convert_element_type | solution.py:681

commit v3 on v2

--- a/solution.py
+++ b/solution.py
@@ -449,8 +449,10 @@
         for index in range(count):
             if index + 1 < count:
                 tops.append(products(index + 1))
+            if index:
+                accumulate(index - 1)
             soften(index, tops[index])
-            accumulate(index)
+        accumulate(count - 1)
 
     def head_of(unit):
         return (1 - at_home) * unit + at_home * (kept + unit // others)

time: 91.5 us -> 91.5 us (level)
  no operation moved by 1% of the time
where the time goes in v3:
time: 91.5 us; the launch traced here: 91.3 us
  Pallas kernels  87.9 us (96%)
  other arithmetic  3.45 us (4%)
    pallas_call x1, Pallas kernels, on_device(): pl.pallas_call(functools.partial(kernel, sections, blocks), out_shape=jax...  87.9 us
    convert_element_type x1, other arithmetic, on_device(): return pl.pallas_call(functools.partial(kernel, sections, blocks), out_sh...  3.45 us

profile of v3, /device:TPU:0, one launch (start us, length us, event | category | flops | bytes accessed | tf_op | source)
XLA Modules:
  0.0 91.3 jit_solution(967463509577255244)
XLA Ops:
  0.0 87.9 %shard_map.37 = bf16[384,2048]{1,0:T(8,128)(2,1)} custom-call(s32[7]{0:T(128)} %lengths_ref.1, bf16[384,3072]{1,0:T(8,128)(2,1)} %bitcast.2, bf16[384,3072]{1,0:T(8,128)(2,1)} %bitcast.3), custom_call_target="tpu_custom_call" | custom-call | flops 10569646080 | bytes 18874368 | tf_op jit(solution)/shard_map/pallas_call | solution.py:632
  87.9 3.4 %convert_element_type.3 = f32[384,2048]{1,0:T(8,128)} convert(bf16[384,2048]{1,0:T(8,128)(2,1)} %shard_map.37) | non-fusion elementwise | flops 786432 | bytes 4718592 | tf_op jit(solution)/shard_map/convert_element_type | solution.py:683
